TPU v7x, 512 devices: a whole 4x4x16 slice. The times are simulated.
512 devices in a mesh: dp: 64 (over y, z), tensor: 8 (over x, core).
Axes of the slice: x: 4, y: 4, z: 16, core: 2. Of those that a mesh axis runs over, the one named last changes fastest.
Arguments:
- queries: bfloat16 [24576, 8192], P(('dp', 'tensor'))
- keys: bfloat16 [24576, 1024], P(('dp', 'tensor')), may hold values from -5 to 5
- values: bfloat16 [24576, 1024], P(('dp', 'tensor')), may hold values from -12 to 12
- ancestors: int32 [256, 6], P('dp'), may hold values from -1 to 255, as said below
Outputs:
- attended: bfloat16 [24576, 8192], P(('dp', 'tensor'))
Inputs may be any that keep to these rules, and one draw needn't show every extreme that they name: Block b consists of tokens b * 96 to (b + 1) * 96 - 1 and lies on dp index b // 4; its family is b % 2 and its copy (b // 2) % 2. Each row lists the chain of ancestors of its block, nearest first (entry k + 1 is the parent of entry k), then -1 in the remaining entries. Ancestors have the block's family and copy and lie on a dp index that differs from the block's by a multiple of 4, at most (15) * 4 away, and with the same remainder modulo 4; those of family 0 lie at lower dp indices, those of family 1 at higher ones. In every tree some block lists 6 ancestors.
All inputs are finite; a program needn't handle non-finite values.
Results may differ from a plain program's by a relative error of at most 0.0032.
Values may be sent and summed in bfloat16 or wider, within the bound.
A program may use at most 64 MiB of HBM per device.

v0:
```python
import math

import jax
import jax.numpy as jnp
from jax import lax
from jax.sharding import PartitionSpec as P

HD = 128
TG = 16


def passed_along(value, axis, by):
    devices = lax.axis_size(axis)
    pairs = [(i, i + by) for i in range(devices) if 0 <= i + by < devices]
    return lax.ppermute(value, axis, pairs)


def block_mask(listed, block_rows):
    listed_live = jnp.repeat(listed >= 0, block_rows)
    row_ids = jnp.arange(block_rows, dtype=jnp.int32)
    causal = row_ids[None, :] <= row_ids[:, None]
    spread_live = jnp.broadcast_to(listed_live[None, :], (block_rows, listed_live.shape[0]))
    return jnp.concatenate([spread_live, causal], axis=1)


def attend(queries_blk, key_rows, value_rows, visible):
    head_size = queries_blk.shape[3]
    scores = jnp.einsum(
        "qkgd,lkd->kgql", queries_blk, key_rows, preferred_element_type=jnp.float32
    ) * (1.0 / math.sqrt(head_size))
    masked = jnp.where(visible, scores, -1e30)
    row_max = jnp.max(masked, axis=-1, keepdims=True)
    weights = jnp.where(visible, jnp.exp(masked - row_max), 0.0)
    weight_sum = jnp.sum(weights, axis=-1)
    combined = jnp.einsum(
        "kgql,lkd->qkgd",
        weights.astype(jnp.bfloat16),
        value_rows,
        preferred_element_type=jnp.float32,
    )
    return (combined / jnp.transpose(weight_sum, (2, 0, 1))[..., None]).astype(jnp.bfloat16)


def local(queries, keys, values, ancestors):
    queries_all, keys_all, values_all = (
        lax.all_to_all(queries, "tensor", split_axis=1, concat_axis=0, tiled=True),
        lax.all_to_all(keys, "tensor", split_axis=1, concat_axis=0, tiled=True),
        lax.all_to_all(values, "tensor", split_axis=1, concat_axis=0, tiled=True),
    )
    token_rows = queries_all.shape[0]
    block_rows = token_rows // 4
    head_size = HD
    kv_width = keys_all.shape[1]
    kv_heads = kv_width // head_size
    q_heads = queries_all.shape[1] // head_size
    group_size = q_heads // kv_heads
    listed_count = ancestors.shape[1]
    spacing = lax.axis_size("dp") // TG
    kv_blocks = jnp.stack([keys_all, values_all]).reshape(2, 2, 2, block_rows, kv_width)
    lower_list = []
    upper_list = []
    for offset in range(1, TG):
        lower_list.append(passed_along(kv_blocks[:, :, 0], "dp", offset * spacing))
        upper_list.append(passed_along(kv_blocks[:, :, 1], "dp", -offset * spacing))
    lower_stack = jnp.stack(lower_list, axis=1)
    upper_stack = jnp.stack(upper_list, axis=1)
    position = lax.axis_index("dp")
    owners = jnp.floor_divide(ancestors, 4)
    head_step = math.gcd(group_size, 4)
    outputs = []
    for slot_index in range(4):
        family = slot_index % 2
        copy_index = slot_index // 2
        if family == 0:
            pick = jnp.clip(jnp.floor_divide(position - owners[slot_index], spacing) - 1, 0, TG - 2)
            picked = jnp.take(lower_stack[:, :, copy_index], pick, axis=1)
        else:
            pick = jnp.clip(jnp.floor_divide(owners[slot_index] - position, spacing) - 1, 0, TG - 2)
            picked = jnp.take(upper_stack[:, :, copy_index], pick, axis=1)
        own = kv_blocks[:, copy_index, family]
        key_rows = jnp.concatenate(
            [
                picked[0].reshape(listed_count * block_rows, kv_heads, head_size),
                own[0].reshape(block_rows, kv_heads, head_size),
            ],
            axis=0,
        )
        value_rows = jnp.concatenate(
            [
                picked[1].reshape(listed_count * block_rows, kv_heads, head_size),
                own[1].reshape(block_rows, kv_heads, head_size),
            ],
            axis=0,
        )
        visible = block_mask(ancestors[slot_index], block_rows)
        queries_blk = queries_all[slot_index * block_rows : (slot_index + 1) * block_rows].reshape(
            block_rows, kv_heads, group_size, head_size
        )
        parts_list = []
        for first_head in range(0, group_size, head_step):
            parts_list.append(
                attend(
                    queries_blk[:, :, first_head : first_head + head_step],
                    key_rows,
                    value_rows,
                    visible,
                )
            )
        outputs.append(jnp.concatenate(parts_list, axis=2).reshape(block_rows, q_heads * head_size))
    attended = jnp.concatenate(outputs, axis=0)
    return lax.all_to_all(attended, "tensor", split_axis=0, concat_axis=1, tiled=True)


def solution(mesh):
    in_specs = (
        P(("dp", "tensor"), None),
        P(("dp", "tensor"), None),
        P(("dp", "tensor"), None),
        P("dp", None),
    )
    out_specs = P(("dp", "tensor"), None)
    return jax.shard_map(local, mesh=mesh, in_specs=in_specs, out_specs=out_specs, check_vma=False)
```

profile of v0, /device:TPU:96, one launch (start us, length us, event | category | flops | bytes accessed | tf_op | source)
XLA Modules:
  0.0 233.3 jit_solution(402764785796053368)
XLA Ops:
  1.5 4.3 %all-to-all-start = ((bf16[48,8,128]{2,0,1:T(8,128)(2,1)}), bf16[48,8,128]{2,0,1:T(8,128)(2,1)S(1)}, u32[]{:S(2)}, u32[]{:S(2)}) async-start(bf16[48,8,128]{2,0,1:T(8,128)(2,1)} %copy_bitcast_fusion.6), calls=%async_computation | async-start | bytes 196608 | tf_op jit(solution)/shard_map/all_to_all | solution.py:47
  13.1 4.8 %all-to-all-start.1 = ((bf16[48,8,128]{2,0,1:T(8,128)(2,1)}), bf16[48,8,128]{2,0,1:T(8,128)(2,1)S(1)}, u32[]{:S(2)}, u32[]{:S(2)}) async-start(bf16[48,8,128]{2,0,1:T(8,128)(2,1)} %copy_bitcast_fusion.5), calls=%async_computation.1 | async-start | bytes 196608 | tf_op jit(solution)/shard_map/all_to_all | solution.py:48
  17.9 5.8 %all-to-all-done.1 = bf16[48,8,128]{2,0,1:T(8,128)(2,1)S(1)} async-done(((bf16[48,8,128]{2,0,1:T(8,128)(2,1)}), bf16[48,8,128]{2,0,1:T(8,128)(2,1)S(1)}, u32[]{:S(2)}, u32[]{:S(2)}) %all-to-all-start.1) | async-done | bytes 98336 | tf_op jit(solution)/shard_map/all_to_all | solution.py:48
  23.7 3.5 %all-to-all-start.2 = ((bf16[48,8,1024]{2,0,1:T(8,128)(2,1)}), bf16[48,8,1024]{2,0,1:T(8,128)(2,1)S(1)}, u32[]{:S(2)}, u32[]{:S(2)}) async-start(bf16[48,8,1024]{2,0,1:T(8,128)(2,1)} %bitcast.492), calls=%async_computation.2 | async-start | bytes 1572864 | tf_op jit(solution)/shard_map/all_to_all | solution.py:46
  27.3 9.1 %collective-permute-start = (bf16[2,2,96,128]{3,2,1,0:T(8,128)(2,1)S(1)}, bf16[2,2,96,128]{3,2,1,0:T(8,128)(2,1)S(1)}, u32[]{:S(2)}, u32[]{:S(2)}) collective-permute-start(bf16[2,2,96,128]{3,2,1,0:T(8,128)(2,1)S(1)} %get-tuple-element.44), channel_id=1, source_target_pairs={{0,32},{8,40},{16,48},{24,56},{32,64},{40,72},{48,80},{56,88},{64,... | collective-permute-start | bytes 294920 | tf_op jit(solution)/shard_map/ppermute | solution.py:15
  36.4 8.2 %collective-permute-start.1 = (bf16[2,2,96,128]{3,2,1,0:T(8,128)(2,1)S(1)}, bf16[2,2,96,128]{3,2,1,0:T(8,128)(2,1)S(1)}, u32[]{:S(2)}, u32[]{:S(2)}) collective-permute-start(bf16[2,2,96,128]{3,2,1,0:T(8,128)(2,1)S(1)} %get-tuple-element.44), channel_id=1, source_target_pairs={{0,64},{8,72},{16,80},{24,88},{32,96},{40,104},{48,112},{56,120},{... | collective-permute-start | bytes 294920 | tf_op jit(solution)/shard_map/ppermute | solution.py:15
  44.6 6.5 %collective-permute-start.2 = (bf16[2,2,96,128]{3,2,1,0:T(8,128)(2,1)S(1)}, bf16[2,2,96,128]{3,2,1,0:T(8,128)(2,1)S(1)}, u32[]{:S(2)}, u32[]{:S(2)}) collective-permute-start(bf16[2,2,96,128]{3,2,1,0:T(8,128)(2,1)S(1)} %get-tuple-element.44), channel_id=1, source_target_pairs={{0,96},{8,104},{16,112},{24,120},{32,128},{40,136},{48,144},{56,15... | collective-permute-start | bytes 294920 | tf_op jit(solution)/shard_map/ppermute | solution.py:15
  51.1 3.5 %collective-permute-start.3 = (bf16[2,2,96,128]{3,2,1,0:T(8,128)(2,1)S(1)}, bf16[2,2,96,128]{3,2,1,0:T(8,128)(2,1)S(1)}, u32[]{:S(2)}, u32[]{:S(2)}) collective-permute-start(bf16[2,2,96,128]{3,2,1,0:T(8,128)(2,1)S(1)} %get-tuple-element.44), channel_id=1, source_target_pairs={{0,128},{8,136},{16,144},{24,152},{32,160},{40,168},{48,176},{56,1... | collective-permute-start | bytes 294920 | tf_op jit(solution)/shard_map/ppermute | solution.py:15
  54.6 5.0 %collective-permute-start.4 = (bf16[2,2,96,128]{3,2,1,0:T(8,128)(2,1)S(1)}, bf16[2,2,96,128]{3,2,1,0:T(8,128)(2,1)S(1)}, u32[]{:S(2)}, u32[]{:S(2)}) collective-permute-start(bf16[2,2,96,128]{3,2,1,0:T(8,128)(2,1)S(1)} %get-tuple-element.44), channel_id=1, source_target_pairs={{0,160},{8,168},{16,176},{24,184},{32,192},{40,200},{48,208},{56,2... | collective-permute-start | bytes 294920 | tf_op jit(solution)/shard_map/ppermute | solution.py:15
  60.9 4.3 %collective-permute-start.5 = (bf16[2,2,96,128]{3,2,1,0:T(8,128)(2,1)S(1)}, bf16[2,2,96,128]{3,2,1,0:T(8,128)(2,1)S(1)}, u32[]{:S(2)}, u32[]{:S(2)}) collective-permute-start(bf16[2,2,96,128]{3,2,1,0:T(8,128)(2,1)S(1)} %get-tuple-element.44), channel_id=1, source_target_pairs={{0,192},{8,200},{16,208},{24,216},{32,224},{40,232},{48,240},{56,2... | collective-permute-start | bytes 294920 | tf_op jit(solution)/shard_map/ppermute | solution.py:15
  71.6 11.4 %collective-permute-start.9 = (bf16[2,2,96,128]{3,2,1,0:T(8,128)(2,1)S(1)}, bf16[2,2,96,128]{3,2,1,0:T(8,128)(2,1)S(1)}, u32[]{:S(2)}, u32[]{:S(2)}) collective-permute-start(bf16[2,2,96,128]{3,2,1,0:T(8,128)(2,1)S(1)} %get-tuple-element.44), channel_id=1, source_target_pairs={{0,320},{8,328},{16,336},{24,344},{32,352},{40,360},{48,368},{56,3... | collective-permute-start | bytes 294920 | tf_op jit(solution)/shard_map/ppermute | solution.py:15
  87.5 4.6 %collective-permute-start.13 = (bf16[2,2,96,128]{3,2,1,0:T(8,128)(2,1)S(1)}, bf16[2,2,96,128]{3,2,1,0:T(8,128)(2,1)S(1)}, u32[]{:S(2)}, u32[]{:S(2)}) collective-permute-start(bf16[2,2,96,128]{3,2,1,0:T(8,128)(2,1)S(1)} %get-tuple-element.44), channel_id=1, source_target_pairs={{0,448},{8,456},{16,464},{24,472},{32,480},{40,488},{48,496},{56,5... | collective-permute-start | bytes 294920 | tf_op jit(solution)/shard_map/ppermute | solution.py:15
  92.2 4.7 %collective-permute-start.14 = (bf16[2,2,96,128]{3,2,1,0:T(8,128)(2,1)S(1)}, bf16[2,2,96,128]{3,2,1,0:T(8,128)(2,1)S(1)}, u32[]{:S(2)}, u32[]{:S(2)}) collective-permute-start(bf16[2,2,96,128]{3,2,1,0:T(8,128)(2,1)S(1)} %get-tuple-element.44), channel_id=1, source_target_pairs={{0,480},{8,488},{16,496},{24,504},{1,481},{9,489},{17,497},{25,505... | collective-permute-start | bytes 294920 | tf_op jit(solution)/shard_map/ppermute | solution.py:15
  99.7 7.5 %collective-permute-done.12 = bf16[2,2,96,128]{3,2,1,0:T(8,128)(2,1)S(1)} collective-permute-done((bf16[2,2,96,128]{3,2,1,0:T(8,128)(2,1)S(1)}, bf16[2,2,96,128]{3,2,1,0:T(8,128)(2,1)S(1)}, u32[]{:S(2)}, u32[]{:S(2)}) %collective-permute-start.12) | collective-permute-done | bytes 98336 | tf_op jit(solution)/shard_map/ppermute | solution.py:15
  111.3 8.5 %collective-permute-done.15 = bf16[2,2,96,128]{3,2,1,0:T(8,128)(2,1)S(1)} collective-permute-done((bf16[2,2,96,128]{3,2,1,0:T(8,128)(2,1)S(1)}, bf16[2,2,96,128]{3,2,1,0:T(8,128)(2,1)S(1)}, u32[]{:S(2)}, u32[]{:S(2)}) %collective-permute-start.15) | collective-permute-done | bytes 98336 | tf_op jit(solution)/shard_map/ppermute | solution.py:15
  121.1 5.9 %collective-permute-done.16 = bf16[2,2,96,128]{3,2,1,0:T(8,128)(2,1)S(1)} collective-permute-done((bf16[2,2,96,128]{3,2,1,0:T(8,128)(2,1)S(1)}, bf16[2,2,96,128]{3,2,1,0:T(8,128)(2,1)S(1)}, u32[]{:S(2)}, u32[]{:S(2)}) %collective-permute-start.16) | collective-permute-done | bytes 98336 | tf_op jit(solution)/shard_map/ppermute | solution.py:15
  128.4 6.2 %collective-permute-done.17 = bf16[2,2,96,128]{3,2,1,0:T(8,128)(2,1)S(1)} collective-permute-done((bf16[2,2,96,128]{3,2,1,0:T(8,128)(2,1)S(1)}, bf16[2,2,96,128]{3,2,1,0:T(8,128)(2,1)S(1)}, u32[]{:S(2)}, u32[]{:S(2)}) %collective-permute-start.17) | collective-permute-done | bytes 98336 | tf_op jit(solution)/shard_map/ppermute | solution.py:15
  141.5 8.7 %collective-permute-done.21 = bf16[2,2,96,128]{3,2,1,0:T(8,128)(2,1)S(1)} collective-permute-done((bf16[2,2,96,128]{3,2,1,0:T(8,128)(2,1)S(1)}, bf16[2,2,96,128]{3,2,1,0:T(8,128)(2,1)S(1)}, u32[]{:S(2)}, u32[]{:S(2)}) %collective-permute-start.21) | collective-permute-done | bytes 98336 | tf_op jit(solution)/shard_map/ppermute | solution.py:15
  154.2 11.5 %collective-permute-done.24 = bf16[2,2,96,128]{3,2,1,0:T(8,128)(2,1)S(1)} collective-permute-done((bf16[2,2,96,128]{3,2,1,0:T(8,128)(2,1)S(1)}, bf16[2,2,96,128]{3,2,1,0:T(8,128)(2,1)S(1)}, u32[]{:S(2)}, u32[]{:S(2)}) %collective-permute-start.24) | collective-permute-done | bytes 98336 | tf_op jit(solution)/shard_map/ppermute | solution.py:15
  167.2 9.6 %collective-permute-done.27 = bf16[2,2,96,128]{3,2,1,0:T(8,128)(2,1)S(1)} collective-permute-done((bf16[2,2,96,128]{3,2,1,0:T(8,128)(2,1)S(1)}, bf16[2,2,96,128]{3,2,1,0:T(8,128)(2,1)S(1)}, u32[]{:S(2)}, u32[]{:S(2)}) %collective-permute-start.27) | collective-permute-done | bytes 98336 | tf_op jit(solution)/shard_map/ppermute | solution.py:15
  176.8 4.7 %collective-permute-done.28 = bf16[2,2,96,128]{3,2,1,0:T(8,128)(2,1)S(1)} collective-permute-done((bf16[2,2,96,128]{3,2,1,0:T(8,128)(2,1)S(1)}, bf16[2,2,96,128]{3,2,1,0:T(8,128)(2,1)S(1)}, u32[]{:S(2)}, u32[]{:S(2)}) %collective-permute-start.28) | collective-permute-done | bytes 98336 | tf_op jit(solution)/shard_map/ppermute | solution.py:15
  181.6 12.5 %collective-permute-done.29 = bf16[2,2,96,128]{3,2,1,0:T(8,128)(2,1)S(1)} collective-permute-done((bf16[2,2,96,128]{3,2,1,0:T(8,128)(2,1)S(1)}, bf16[2,2,96,128]{3,2,1,0:T(8,128)(2,1)S(1)}, u32[]{:S(2)}, u32[]{:S(2)}) %collective-permute-start.29) | collective-permute-done | bytes 98336 | tf_op jit(solution)/shard_map/ppermute | solution.py:15
  195.7 2.4 %gather_fusion.1 = bf16[6,2,96,128]{3,2,1,0:T(8,128)(2,1)} fusion(bf16[2,15,96,128]{3,2,0,1:T(8,128)(2,1)} %get-tuple-element.24, s32[1024]{0:T(1024)S(1)} %pad_clamp_fusion.2), kind=kCustom, calls=%fused_computation.1.clone | custom fusion | bytes 589848 | tf_op jit(solution)/shard_map/jit(_take)/gather | solution.py:79
  214.8 17.5 %all_to_all.67 = bf16[8,48,1024]{2,1,0:T(8,128)(2,1)S(1)} all-to-all(bf16[8,48,1024]{2,1,0:T(8,128)(2,1)S(1)} %bitcast.498), channel_id=1, replica_groups=mesh['dp'=64,'tensor'=8] {'tensor'}, dimensions={0} | all-to-all | bytes 1572864 | tf_op jit(solution)/shard_map/all_to_all | solution.py:111
  (183 shorter events, 61.2 us)
Async XLA Ops:
  23.7 177.6 %all-to-all-start.2 = ((bf16[48,8,1024]{2,0,1:T(8,128)(2,1)}), bf16[48,8,1024]{2,0,1:T(8,128)(2,1)S(1)}, u32[]{:S(2)}, u32[]{:S(2)}) async-start(bf16[48,8,1024]{2,0,1:T(8,128)(2,1)} %bitcast.492), calls=%async_computation.2 | async-start | bytes 1572864 | tf_op jit(solution)/shard_map/all_to_all | solution.py:46
  27.3 33.6 %collective-permute-start = (bf16[2,2,96,128]{3,2,1,0:T(8,128)(2,1)S(1)}, bf16[2,2,96,128]{3,2,1,0:T(8,128)(2,1)S(1)}, u32[]{:S(2)}, u32[]{:S(2)}) collective-permute-start(bf16[2,2,96,128]{3,2,1,0:T(8,128)(2,1)S(1)} %get-tuple-element.44), channel_id=1, source_target_pairs={{0,32},{8,40},{16,48},{24,56},{32,64},{40,72},{48,80},{56,88},{64,... | collective-permute-start | bytes 294920 | tf_op jit(solution)/shard_map/ppermute | solution.py:15
  36.4 28.9 %collective-permute-start.1 = (bf16[2,2,96,128]{3,2,1,0:T(8,128)(2,1)S(1)}, bf16[2,2,96,128]{3,2,1,0:T(8,128)(2,1)S(1)}, u32[]{:S(2)}, u32[]{:S(2)}) collective-permute-start(bf16[2,2,96,128]{3,2,1,0:T(8,128)(2,1)S(1)} %get-tuple-element.44), channel_id=1, source_target_pairs={{0,64},{8,72},{16,80},{24,88},{32,96},{40,104},{48,112},{56,120},{... | collective-permute-start | bytes 294920 | tf_op jit(solution)/shard_map/ppermute | solution.py:15
  44.6 22.0 %collective-permute-start.2 = (bf16[2,2,96,128]{3,2,1,0:T(8,128)(2,1)S(1)}, bf16[2,2,96,128]{3,2,1,0:T(8,128)(2,1)S(1)}, u32[]{:S(2)}, u32[]{:S(2)}) collective-permute-start(bf16[2,2,96,128]{3,2,1,0:T(8,128)(2,1)S(1)} %get-tuple-element.44), channel_id=1, source_target_pairs={{0,96},{8,104},{16,112},{24,120},{32,128},{40,136},{48,144},{56,15... | collective-permute-start | bytes 294920 | tf_op jit(solution)/shard_map/ppermute | solution.py:15
  60.9 22.2 %collective-permute-start.5 = (bf16[2,2,96,128]{3,2,1,0:T(8,128)(2,1)S(1)}, bf16[2,2,96,128]{3,2,1,0:T(8,128)(2,1)S(1)}, u32[]{:S(2)}, u32[]{:S(2)}) collective-permute-start(bf16[2,2,96,128]{3,2,1,0:T(8,128)(2,1)S(1)} %get-tuple-element.44), channel_id=1, source_target_pairs={{0,192},{8,200},{16,208},{24,216},{32,224},{40,232},{48,240},{56,2... | collective-permute-start | bytes 294920 | tf_op jit(solution)/shard_map/ppermute | solution.py:15
  65.3 19.5 %collective-permute-start.6 = (bf16[2,2,96,128]{3,2,1,0:T(8,128)(2,1)S(1)}, bf16[2,2,96,128]{3,2,1,0:T(8,128)(2,1)S(1)}, u32[]{:S(2)}, u32[]{:S(2)}) collective-permute-start(bf16[2,2,96,128]{3,2,1,0:T(8,128)(2,1)S(1)} %get-tuple-element.44), channel_id=1, source_target_pairs={{0,224},{8,232},{16,240},{24,248},{32,256},{40,264},{48,272},{56,2... | collective-permute-start | bytes 294920 | tf_op jit(solution)/shard_map/ppermute | solution.py:15
  66.7 19.5 %collective-permute-start.7 = (bf16[2,2,96,128]{3,2,1,0:T(8,128)(2,1)S(1)}, bf16[2,2,96,128]{3,2,1,0:T(8,128)(2,1)S(1)}, u32[]{:S(2)}, u32[]{:S(2)}) collective-permute-start(bf16[2,2,96,128]{3,2,1,0:T(8,128)(2,1)S(1)} %get-tuple-element.44), channel_id=1, source_target_pairs={{0,256},{8,264},{16,272},{24,280},{32,288},{40,296},{48,304},{56,3... | collective-permute-start | bytes 294920 | tf_op jit(solution)/shard_map/ppermute | solution.py:15
  68.0 19.5 %collective-permute-start.8 = (bf16[2,2,96,128]{3,2,1,0:T(8,128)(2,1)S(1)}, bf16[2,2,96,128]{3,2,1,0:T(8,128)(2,1)S(1)}, u32[]{:S(2)}, u32[]{:S(2)}) collective-permute-start(bf16[2,2,96,128]{3,2,1,0:T(8,128)(2,1)S(1)} %get-tuple-element.44), channel_id=1, source_target_pairs={{0,288},{8,296},{16,304},{24,312},{32,320},{40,328},{48,336},{56,3... | collective-permute-start | bytes 294920 | tf_op jit(solution)/shard_map/ppermute | solution.py:15
  71.6 20.6 %collective-permute-start.9 = (bf16[2,2,96,128]{3,2,1,0:T(8,128)(2,1)S(1)}, bf16[2,2,96,128]{3,2,1,0:T(8,128)(2,1)S(1)}, u32[]{:S(2)}, u32[]{:S(2)}) collective-permute-start(bf16[2,2,96,128]{3,2,1,0:T(8,128)(2,1)S(1)} %get-tuple-element.44), channel_id=1, source_target_pairs={{0,320},{8,328},{16,336},{24,344},{32,352},{40,360},{48,368},{56,3... | collective-permute-start | bytes 294920 | tf_op jit(solution)/shard_map/ppermute | solution.py:15
  86.2 21.0 %collective-permute-start.12 = (bf16[2,2,96,128]{3,2,1,0:T(8,128)(2,1)S(1)}, bf16[2,2,96,128]{3,2,1,0:T(8,128)(2,1)S(1)}, u32[]{:S(2)}, u32[]{:S(2)}) collective-permute-start(bf16[2,2,96,128]{3,2,1,0:T(8,128)(2,1)S(1)} %get-tuple-element.44), channel_id=1, source_target_pairs={{0,416},{8,424},{16,432},{24,440},{32,448},{40,456},{48,464},{56,4... | collective-permute-start | bytes 294920 | tf_op jit(solution)/shard_map/ppermute | solution.py:15
  87.5 20.9 %collective-permute-start.13 = (bf16[2,2,96,128]{3,2,1,0:T(8,128)(2,1)S(1)}, bf16[2,2,96,128]{3,2,1,0:T(8,128)(2,1)S(1)}, u32[]{:S(2)}, u32[]{:S(2)}) collective-permute-start(bf16[2,2,96,128]{3,2,1,0:T(8,128)(2,1)S(1)} %get-tuple-element.44), channel_id=1, source_target_pairs={{0,448},{8,456},{16,464},{24,472},{32,480},{40,488},{48,496},{56,5... | collective-permute-start | bytes 294920 | tf_op jit(solution)/shard_map/ppermute | solution.py:15
  92.2 17.6 %collective-permute-start.14 = (bf16[2,2,96,128]{3,2,1,0:T(8,128)(2,1)S(1)}, bf16[2,2,96,128]{3,2,1,0:T(8,128)(2,1)S(1)}, u32[]{:S(2)}, u32[]{:S(2)}) collective-permute-start(bf16[2,2,96,128]{3,2,1,0:T(8,128)(2,1)S(1)} %get-tuple-element.44), channel_id=1, source_target_pairs={{0,480},{8,488},{16,496},{24,504},{1,481},{9,489},{17,497},{25,505... | collective-permute-start | bytes 294920 | tf_op jit(solution)/shard_map/ppermute | solution.py:15
  97.0 22.8 %collective-permute-start.15 = (bf16[2,2,96,128]{3,2,1,0:T(8,128)(2,1)S(1)}, bf16[2,2,96,128]{3,2,1,0:T(8,128)(2,1)S(1)}, u32[]{:S(2)}, u32[]{:S(2)}) collective-permute-start(bf16[2,2,96,128]{3,2,1,0:T(8,128)(2,1)S(1)} %get-tuple-element.45), channel_id=1, source_target_pairs={{32,0},{40,8},{48,16},{56,24},{64,32},{72,40},{80,48},{88,56},{96,... | collective-permute-start | bytes 294920 | tf_op jit(solution)/shard_map/ppermute | solution.py:15
  98.3 28.7 %collective-permute-start.16 = (bf16[2,2,96,128]{3,2,1,0:T(8,128)(2,1)S(1)}, bf16[2,2,96,128]{3,2,1,0:T(8,128)(2,1)S(1)}, u32[]{:S(2)}, u32[]{:S(2)}) collective-permute-start(bf16[2,2,96,128]{3,2,1,0:T(8,128)(2,1)S(1)} %get-tuple-element.45), channel_id=1, source_target_pairs={{64,0},{72,8},{80,16},{88,24},{96,32},{104,40},{112,48},{120,56},{... | collective-permute-start | bytes 294920 | tf_op jit(solution)/shard_map/ppermute | solution.py:15
  107.2 27.4 %collective-permute-start.17 = (bf16[2,2,96,128]{3,2,1,0:T(8,128)(2,1)S(1)}, bf16[2,2,96,128]{3,2,1,0:T(8,128)(2,1)S(1)}, u32[]{:S(2)}, u32[]{:S(2)}) collective-permute-start(bf16[2,2,96,128]{3,2,1,0:T(8,128)(2,1)S(1)} %get-tuple-element.45), channel_id=1, source_target_pairs={{96,0},{104,8},{112,16},{120,24},{128,32},{136,40},{144,48},{152,5... | collective-permute-start | bytes 294920 | tf_op jit(solution)/shard_map/ppermute | solution.py:15
  108.5 27.4 %collective-permute-start.18 = (bf16[2,2,96,128]{3,2,1,0:T(8,128)(2,1)S(1)}, bf16[2,2,96,128]{3,2,1,0:T(8,128)(2,1)S(1)}, u32[]{:S(2)}, u32[]{:S(2)}) collective-permute-start(bf16[2,2,96,128]{3,2,1,0:T(8,128)(2,1)S(1)} %get-tuple-element.45), channel_id=1, source_target_pairs={{128,0},{136,8},{144,16},{152,24},{160,32},{168,40},{176,48},{184,... | collective-permute-start | bytes 294920 | tf_op jit(solution)/shard_map/ppermute | solution.py:15
  109.8 27.4 %collective-permute-start.19 = (bf16[2,2,96,128]{3,2,1,0:T(8,128)(2,1)S(1)}, bf16[2,2,96,128]{3,2,1,0:T(8,128)(2,1)S(1)}, u32[]{:S(2)}, u32[]{:S(2)}) collective-permute-start(bf16[2,2,96,128]{3,2,1,0:T(8,128)(2,1)S(1)} %get-tuple-element.45), channel_id=1, source_target_pairs={{160,0},{168,8},{176,16},{184,24},{192,32},{200,40},{208,48},{216,... | collective-permute-start | bytes 294920 | tf_op jit(solution)/shard_map/ppermute | solution.py:15
  119.8 20.4 %collective-permute-start.20 = (bf16[2,2,96,128]{3,2,1,0:T(8,128)(2,1)S(1)}, bf16[2,2,96,128]{3,2,1,0:T(8,128)(2,1)S(1)}, u32[]{:S(2)}, u32[]{:S(2)}) collective-permute-start(bf16[2,2,96,128]{3,2,1,0:T(8,128)(2,1)S(1)} %get-tuple-element.45), channel_id=1, source_target_pairs={{192,0},{200,8},{208,16},{216,24},{224,32},{232,40},{240,48},{248,... | collective-permute-start | bytes 294920 | tf_op jit(solution)/shard_map/ppermute | solution.py:15
  127.0 23.1 %collective-permute-start.21 = (bf16[2,2,96,128]{3,2,1,0:T(8,128)(2,1)S(1)}, bf16[2,2,96,128]{3,2,1,0:T(8,128)(2,1)S(1)}, u32[]{:S(2)}, u32[]{:S(2)}) collective-permute-start(bf16[2,2,96,128]{3,2,1,0:T(8,128)(2,1)S(1)} %get-tuple-element.45), channel_id=1, source_target_pairs={{224,0},{232,8},{240,16},{248,24},{256,32},{264,40},{272,48},{280,... | collective-permute-start | bytes 294920 | tf_op jit(solution)/shard_map/ppermute | solution.py:15
  137.3 28.4 %collective-permute-start.24 = (bf16[2,2,96,128]{3,2,1,0:T(8,128)(2,1)S(1)}, bf16[2,2,96,128]{3,2,1,0:T(8,128)(2,1)S(1)}, u32[]{:S(2)}, u32[]{:S(2)}) collective-permute-start(bf16[2,2,96,128]{3,2,1,0:T(8,128)(2,1)S(1)} %get-tuple-element.45), channel_id=1, source_target_pairs={{320,0},{328,8},{336,16},{344,24},{352,32},{360,40},{368,48},{376,... | collective-permute-start | bytes 294920 | tf_op jit(solution)/shard_map/ppermute | solution.py:15
  140.2 26.9 %collective-permute-start.25 = (bf16[2,2,96,128]{3,2,1,0:T(8,128)(2,1)S(1)}, bf16[2,2,96,128]{3,2,1,0:T(8,128)(2,1)S(1)}, u32[]{:S(2)}, u32[]{:S(2)}) collective-permute-start(bf16[2,2,96,128]{3,2,1,0:T(8,128)(2,1)S(1)} %get-tuple-element.45), channel_id=1, source_target_pairs={{352,0},{360,8},{368,16},{376,24},{384,32},{392,40},{400,48},{408,... | collective-permute-start | bytes 294920 | tf_op jit(solution)/shard_map/ppermute | solution.py:15
  151.5 25.3 %collective-permute-start.27 = (bf16[2,2,96,128]{3,2,1,0:T(8,128)(2,1)S(1)}, bf16[2,2,96,128]{3,2,1,0:T(8,128)(2,1)S(1)}, u32[]{:S(2)}, u32[]{:S(2)}) collective-permute-start(bf16[2,2,96,128]{3,2,1,0:T(8,128)(2,1)S(1)} %get-tuple-element.45), channel_id=1, source_target_pairs={{416,0},{424,8},{432,16},{440,24},{448,32},{456,40},{464,48},{472,... | collective-permute-start | bytes 294920 | tf_op jit(solution)/shard_map/ppermute | solution.py:15
  152.8 28.7 %collective-permute-start.28 = (bf16[2,2,96,128]{3,2,1,0:T(8,128)(2,1)S(1)}, bf16[2,2,96,128]{3,2,1,0:T(8,128)(2,1)S(1)}, u32[]{:S(2)}, u32[]{:S(2)}) collective-permute-start(bf16[2,2,96,128]{3,2,1,0:T(8,128)(2,1)S(1)} %get-tuple-element.45), channel_id=1, source_target_pairs={{448,0},{456,8},{464,16},{472,24},{480,32},{488,40},{496,48},{504,... | collective-permute-start | bytes 294920 | tf_op jit(solution)/shard_map/ppermute | solution.py:15
  165.6 28.4 %collective-permute-start.29 = (bf16[2,2,96,128]{3,2,1,0:T(8,128)(2,1)S(1)}, bf16[2,2,96,128]{3,2,1,0:T(8,128)(2,1)S(1)}, u32[]{:S(2)}, u32[]{:S(2)}) collective-permute-start(bf16[2,2,96,128]{3,2,1,0:T(8,128)(2,1)S(1)} %get-tuple-element.45), channel_id=1, source_target_pairs={{480,0},{488,8},{496,16},{504,24},{481,1},{489,9},{497,17},{505,25... | collective-permute-start | bytes 294920 | tf_op jit(solution)/shard_map/ppermute | solution.py:15
  (23 other events, 147.9 us)
where the time goes:
time: 235 us; the launch traced here: 233 us
  starting transfers between devices  97.8 us (42%)
  waiting for transfers between devices  84.9 us (36%)
  local copies, waits for them, and re-layouts  18.1 us (8%)
  blocking collectives  17.5 us (7%)
  other arithmetic  7.07 us (3%)
  matrix products  6.87 us (3%)
    ppermute x30, starting transfers between devices, passed_along(): return lax.ppermute(value, axis, pairs)  85.1 us
    ppermute x30, waiting for transfers between devices, passed_along(): return lax.ppermute(value, axis, pairs)  79.1 us
    all_to_all x1, blocking collectives, local(): lax.all_to_all(attended, 'tensor', split_axis=0, concat_axis=1, tiled=True)  17.5 us
    all_to_all x1, waiting for transfers between devices, local(): lax.all_to_all(values, 'tensor', split_axis=1, concat_axis=0, tiled=True)  5.79 us
    all_to_all x1, starting transfers between devices, local(): lax.all_to_all(values, 'tensor', split_axis=1, concat_axis=0, tiled=True)  4.82 us
  transfers between devices with their start and end apart: 33, of which 12 were waited for; matrix products, arithmetic and copies ran while one was open for 7% of the time, Pallas kernels for 0%

commit v1 on v0

v1 whole, which is shorter than its diff:
```python
import functools
import math

import jax
import jax.numpy as jnp
from jax import lax
from jax.experimental import pallas as pl
from jax.experimental.pallas import tpu as pltpu
from jax.sharding import PartitionSpec as P

HD = 128
NODE = 96
HALF = 48
ANC = 6
KEYS = (ANC + 1) * NODE
GROUP = 8
HEADS = 4
JOINT = 4
MESH = pl.DeviceIdType.MESH
EXP_SCALE = math.log2(math.e) / math.sqrt(HD)


def kernel(q_ref, k_ref, v_ref, anc_ref, out_ref, kv0, kv1, kv2, kv3, q_s, o_s, bias_s,
           own_l, own_s, own_r, q_sem, zs, zf, zr, zo, ys, yr, os_, or_, ol):
    kv = (kv0, kv1, kv2, kv3)
    dp, t = lax.axis_index("dp"), lax.axis_index("tensor")
    x, c = t // 2, t % 2
    y, w, g = dp // 16, (dp % 16) // 4, dp % 4
    f = x % 2
    Y = y + f * (3 - 2 * y)
    W = w + f * (3 - 2 * w)

    def dev(row, col):
        yy = row + f * (3 - 2 * row)
        ww = col + f * (3 - 2 * col)
        return (yy * 16 + ww * 4 + g, t)

    cols = [lax.rem(W + i, 4) for i in range(4)]
    me = Y * 4 + W
    sibling = (dp, x * 2 + 1 - c)
    z_next, z_prev = dev(Y, cols[1]), dev(Y, cols[3])
    y_next, y_prev = dev(lax.rem(Y + 1, 4), W), dev(lax.rem(Y + 3, 4), W)
    mine = pl.ds(pl.multiple_of(c * HALF, 16), HALF)
    theirs = pl.ds(pl.multiple_of((1 - c) * HALF, 16), HALF)

    def lanes(start, size):
        return pl.ds(pl.multiple_of(start, 128), size)

    own = []
    for h in range(HEADS):
        for i, ref in enumerate((k_ref, v_ref)):
            n = h * 2 + i
            local = pltpu.make_async_copy(
                ref.at[:, lanes(c * 512 + h * HD, HD)], kv[h].at[me, i, mine], own_l.at[n])
            remote = pltpu.make_async_remote_copy(
                ref.at[:, lanes((1 - c) * 512 + h * HD, HD)], kv[h].at[me, i, mine],
                own_s.at[n], own_r.at[n], device_id=sibling, device_id_type=MESH)
            local.start()
            own.append((local, remote))
    q_local = pltpu.make_async_copy(q_ref.at[:, lanes(c * 4096, 4096)], q_s.at[mine], q_sem.at[0])
    q_remote = pltpu.make_async_remote_copy(
        q_ref.at[:, lanes((1 - c) * 4096, 4096)], q_s.at[mine], q_sem.at[1], q_sem.at[2],
        device_id=sibling, device_id_type=MESH)
    q_local.start()

    barrier = pltpu.get_barrier_semaphore()
    for partner in (sibling, z_next, z_prev, y_next, y_prev):
        pl.semaphore_signal(barrier, inc=1, device_id=partner, device_id_type=MESH)
    pl.semaphore_wait(barrier, 5)

    for _, remote in own:
        remote.start()
    q_remote.start()

    sent = []

    def send(src, dst, s_sem, r_sem, to, when=None):
        copy = pltpu.make_async_remote_copy(src, dst, s_sem, r_sem, device_id=to, device_id_type=MESH)
        if when is None:
            copy.start()
        else:
            pl.when(when)(copy.start)
        sent.append((copy, when))

    def arrived(ref, sem, when=None):
        copy = pltpu.make_async_remote_copy(ref, ref, sem, sem, device_id=sibling, device_id_type=MESH)
        if when is None:
            copy.wait_recv()
        else:
            pl.when(when)(copy.wait_recv)

    def y_block(h, row, i, to, n, when):
        slot = row * 4 + cols[i]
        send(kv[h].at[slot], kv[h].at[slot], ys.at[h, n], yr.at[h, slot], to, when)

    def y_own(h, i):
        y_block(h, Y, i, y_next, i, Y < 3)
        if i % 2 == 0:
            y_block(h, Y, i, y_prev, 4 + i, Y == 0)
        else:
            y_block(h, Y, i, y_prev, 4 + i, Y < 2)

    def y_arrived(h, row, i, when):
        slot = row * 4 + cols[i]
        arrived(kv[h].at[slot], yr.at[h, slot], when)

    def send_own(h):
        for i in range(2):
            local, remote = own[h * 2 + i]
            local.wait()
            remote.wait_recv()
        src = kv[h].at[me]
        send(src, src, zs.at[h, 0], zr.at[h, 0], z_next)
        send(src, src, zs.at[h, 1], zr.at[h, 1], z_prev)
        y_own(h, 0)

    def z_near(h):
        for n, i, to in ((0, 3, z_next), (1, 1, z_prev)):
            slot = kv[h].at[Y * 4 + cols[i]]
            arrived(slot, zr.at[h, n])
            send(slot.at[n], slot.at[n], zf.at[h, n], zo.at[h, n], to)
            y_own(h, i)

    def z_far(h):
        slot = kv[h].at[Y * 4 + cols[2]]
        for n in range(2):
            arrived(slot.at[n], zo.at[h, n])
        y_own(h, 2)

    def relay(h, i):
        if i % 2 == 0:
            y_arrived(h, 1, i, Y == 2)
            y_block(h, 1, i, y_next, 8 + i, Y == 2)
        else:
            y_arrived(h, 1, i, Y == 0)
            y_block(h, 1, i, y_prev, 8 + i, Y == 0)
        y_arrived(h, 0, i, Y == 3)
        y_block(h, 0, i, y_prev, 8 + i, Y == 3)

    def rest(h):
        for i in range(4):
            y_arrived(h, 0, i, Y == 1)
            if i % 2 == 1:
                y_arrived(h, 1, i, Y == 2)
            y_arrived(h, 0, i, Y == 2)
            y_arrived(h, 2, i, Y == 3)
            y_arrived(h, 1, i, Y == 3)

    listed = [anc_ref[x, i] for i in range(ANC)]
    places = []
    for a in listed:
        a0 = jnp.maximum(a, 0)
        ay, aw = a0 >> 6, (a0 >> 4) & 3
        ay = ay + f * (3 - 2 * ay)
        aw = aw + f * (3 - 2 * aw)
        places.append(jnp.where(a >= 0, ay * 4 + aw, me))
    places.append(me)

    def build_bias():
        rows = lax.broadcasted_iota(jnp.int32, (NODE, KEYS), 0)
        at = lax.broadcasted_iota(jnp.int32, (NODE, KEYS), 1)
        bias = jnp.where(at - ANC * NODE > rows, -1e30, 0.0)
        for i, a in enumerate(listed):
            inside = (at >= NODE * i) & (at < NODE * (i + 1))
            bias = jnp.where(inside, jnp.where(a >= 0, 0.0, -1e30), bias)
        bias_s[...] = bias

    out_copies = []

    def attend(h):
        keys = jnp.concatenate([kv[h][s, 0] for s in places], axis=0)
        values = jnp.concatenate([kv[h][s, 1] for s in places], axis=0)
        for first in range(0, GROUP, JOINT):
            at = [(h * GROUP + first + j) * HD for j in range(JOINT)]
            queries = jnp.concatenate([q_s[:, a:a + HD] for a in at], axis=0)
            scores = lax.dot_general(queries, keys, (((1,), (1,)), ((), ())), preferred_element_type=jnp.float32)
            scores = (scores.reshape(JOINT, NODE, KEYS) + bias_s[...][None]).reshape(JOINT * NODE, KEYS)
            top = jnp.max(scores, axis=-1, keepdims=True)
            weights = jnp.exp2((scores - top) * EXP_SCALE)
            total = jnp.sum(weights, axis=-1, keepdims=True)
            mixed = jnp.dot(weights.astype(jnp.bfloat16), values, preferred_element_type=jnp.float32)
            mixed = (mixed / total).astype(jnp.bfloat16)
            for j in range(JOINT):
                o_s[:, at[j]:at[j] + HD] = mixed[j * NODE:(j + 1) * NODE]
        width = GROUP * HD
        there = out_ref.at[:, lanes(c * 4096 + h * width, width)]
        local = pltpu.make_async_copy(o_s.at[mine, pl.ds(h * width, width)], there, ol.at[h])
        remote = pltpu.make_async_remote_copy(
            o_s.at[theirs, pl.ds(h * width, width)], there, os_.at[h], or_.at[h],
            device_id=sibling, device_id_type=MESH)
        local.start()
        remote.start()
        out_copies.append((local, remote))

    def relays(h):
        for i in (0, 3, 1, 2):
            relay(h, i)

    send_own(0)
    send_own(1)
    build_bias()
    q_local.wait()
    q_remote.wait_recv()
    z_near(0)
    send_own(2)
    z_near(1)
    z_far(0)
    send_own(3)
    relays(0)
    z_near(2)
    z_far(1)
    rest(0)
    attend(0)
    relays(1)
    z_near(3)
    z_far(2)
    rest(1)
    attend(1)
    relays(2)
    z_far(3)
    rest(2)
    attend(2)
    relays(3)
    rest(3)
    attend(3)

    for _, remote in own:
        remote.wait_send()
    q_remote.wait_send()
    for copy, when in sent:
        if when is None:
            copy.wait_send()
        else:
            pl.when(when)(copy.wait_send)
    for local, remote in out_copies:
        local.wait()
        remote.wait()


def local(queries, keys, values, ancestors):
    kv = pltpu.VMEM((16, 2, NODE, HD), jnp.bfloat16)
    dma = pltpu.SemaphoreType.DMA
    anywhere = pl.BlockSpec(memory_space=pl.ANY)
    return pl.pallas_call(
        kernel,
        out_shape=jax.ShapeDtypeStruct((HALF, 8192), jnp.bfloat16),
        in_specs=[anywhere, anywhere, anywhere, pl.BlockSpec(memory_space=pltpu.SMEM)],
        out_specs=anywhere,
        scratch_shapes=[
            kv, kv, kv, kv,
            pltpu.VMEM((NODE, 4096), jnp.bfloat16),
            pltpu.VMEM((NODE, 4096), jnp.bfloat16),
            pltpu.VMEM((NODE, KEYS), jnp.float32),
            dma((8,)), dma((8,)), dma((8,)), dma((3,)),
            dma((4, 2)), dma((4, 2)), dma((4, 2)), dma((4, 2)),
            dma((4, 12)), dma((4, 16)),
            dma((4,)), dma((4,)), dma((4,)),
        ],
        compiler_params=pltpu.CompilerParams(
            collective_id=0, has_side_effects=True, vmem_limit_bytes=48 << 20),
        cost_estimate=pl.CostEstimate(flops=2 * 2 * 96 * 32 * 672 * 128, bytes_accessed=4 << 20, transcendentals=96 * 32 * 672),
        name="tree_attention",
    )(queries, keys, values, ancestors)


def solution(mesh):
    split = P(("dp", "tensor"), None)
    return jax.shard_map(
        local, mesh=mesh, in_specs=(split, split, split, P("dp", None)), out_specs=split, check_vma=False)
```

time: 235 us -> 71.3 us (0.30)
  the two profiles are of different devices: /device:TPU:96 before, /device:TPU:11 now
where the time goes in v1:
time: 71.3 us; the launch traced here: 71.1 us
  Pallas kernels  66.6 us (93%)
  local copies, waits for them, and re-layouts  4.48 us (6%)
    pallas_call x1, Pallas kernels, local(): pl.pallas_call(kernel, out_shape=jax.ShapeDtypeStruct((HALF, 8192), jnp.b...  66.6 us
    unnamed x9, local copies, waits for them, and re-layouts  4.48 us

profile of v1, /device:TPU:11, one launch (start us, length us, event | category | flops | bytes accessed | tf_op | source)
XLA Modules:
  0.0 71.1 jit_solution(4908328423522931058)
XLA Ops:
  0.0 0.0 copy-start
  0.0 1.1 %copy-done = bf16[48,8192]{1,0:T(8,128)(2,1)S(1)} copy-done((bf16[48,8192]{1,0:T(8,128)(2,1)S(1)}, bf16[48,8192]{1,0:T(8,128)(2,1)}, u32[]{:S(2)}) %copy-start) | copy-done | bytes 786456
  1.1 0.0 copy-start.1
  1.1 0.9 %copy-done.1 = bf16[48,1024]{1,0:T(8,128)(2,1)S(1)} copy-done((bf16[48,1024]{1,0:T(8,128)(2,1)S(1)}, bf16[48,1024]{1,0:T(8,128)(2,1)}, u32[]{:S(2)}) %copy-start.1) | copy-done | bytes 98328
  2.0 0.0 copy-start.2
  2.0 0.9 %copy-done.2 = bf16[48,1024]{1,0:T(8,128)(2,1)S(1)} copy-done((bf16[48,1024]{1,0:T(8,128)(2,1)S(1)}, bf16[48,1024]{1,0:T(8,128)(2,1)}, u32[]{:S(2)}) %copy-start.2) | copy-done | bytes 98328
  2.9 0.0 copy-start.3
  2.9 0.7 copy-done.3
  3.6 66.6 %tree_attention.1 = bf16[48,8192]{1,0:T(8,128)(2,1)S(1)} custom-call(bf16[48,8192]{1,0:T(8,128)(2,1)S(1)} %copy-done, bf16[48,1024]{1,0:T(8,128)(2,1)S(1)} %copy-done.1, bf16[48,1024]{1,0:T(8,128)(2,1)S(1)} %copy-done.2, s32[4,6]{1,0:T(4,128)S(1)} %copy-done.3), custom_call_target="tpu_custom_call" | custom-call | flops 1056964608 | bytes 4194304 | tf_op jit(solution)/shard_map/tree_attention/pallas_call | solution.py:244
  70.2 0.9 %copy.6 = bf16[48,8192]{1,0:T(8,128)(2,1)} copy(bf16[48,8192]{1,0:T(8,128)(2,1)S(1)} %tree_attention.1) | data formatting | bytes 1572864
Async XLA Ops:
  0.0 1.1 %copy-start = (bf16[48,8192]{1,0:T(8,128)(2,1)S(1)}, bf16[48,8192]{1,0:T(8,128)(2,1)}, u32[]{:S(2)}) copy-start(bf16[48,8192]{1,0:T(8,128)(2,1)} %q_ref.1) | copy-start | bytes 2359300
  1.1 0.9 %copy-start.1 = (bf16[48,1024]{1,0:T(8,128)(2,1)S(1)}, bf16[48,1024]{1,0:T(8,128)(2,1)}, u32[]{:S(2)}) copy-start(bf16[48,1024]{1,0:T(8,128)(2,1)} %k_ref.1) | copy-start | bytes 294916
  2.0 0.9 %copy-start.2 = (bf16[48,1024]{1,0:T(8,128)(2,1)S(1)}, bf16[48,1024]{1,0:T(8,128)(2,1)}, u32[]{:S(2)}) copy-start(bf16[48,1024]{1,0:T(8,128)(2,1)} %v_ref.1) | copy-start | bytes 294916
  2.9 0.7 copy-start.3

commit v2 on v1

v2 whole, which is shorter than its diff:
```python
import math

import jax
import jax.numpy as jnp
from jax import lax
from jax.experimental import pallas as pl
from jax.experimental.pallas import tpu as pltpu
from jax.sharding import PartitionSpec as P

HD = 128
NODE = 96
HALF = 48
ANC = 6
KEYS = (ANC + 1) * NODE
GROUP = 8
JOINT = 4
MESH = pl.DeviceIdType.MESH
EXP_SCALE = math.log2(math.e) / math.sqrt(HD)
UNITS = ((0, 0), (1, 0), (1, 1), (0, 1))


def kernel(q_ref, k_ref, v_ref, anc_hbm, out_ref, anc_ref, anc_sem, kv0, kv1, kv2, kv3, q_s, o_s, bias_s,
           kv_l, kv_s, kv_r, q_l, q_t, q_r, zs, zf, zr, zo, ys, yr, o_l, o_t, o_r):
    kv = (kv0, kv1, kv2, kv3)
    dp, t = lax.axis_index("dp"), lax.axis_index("tensor")
    x, c = t // 2, t % 2
    y, w, g = dp // 16, (dp % 16) // 4, dp % 4
    px = x + 1 - 2 * (x % 2)
    r = t % 4

    fam = [x % 2, px % 2]
    rows = [y + f * (3 - 2 * y) for f in fam]
    cols = [w + f * (3 - 2 * w) for f in fam]
    me = [rows[b] * 4 + cols[b] for b in range(2)]

    def dev(b, row, col):
        yy = row + fam[b] * (3 - 2 * row)
        ww = col + fam[b] * (3 - 2 * col)
        return (yy * 16 + ww * 4 + g, t)

    def col_at(b, i):
        return lax.rem(cols[b] + i, 4)

    sibling = (dp, x * 2 + 1 - c)
    across = [(dp, px * 2 + cc) for cc in range(2)]
    mine = pl.ds(pl.multiple_of(c * HALF, 16), HALF)
    theirs = pl.ds(pl.multiple_of((1 - c) * HALF, 16), HALF)

    def lanes(start, size):
        return pl.ds(pl.multiple_of(start, 128), size)

    def remote(src, dst, s_sem, r_sem, to):
        return pltpu.make_async_remote_copy(src, dst, s_sem, r_sem, device_id=to, device_id_type=MESH)

    sent = []

    def send(src, dst, s_sem, r_sem, to, when=None):
        copy = remote(src, dst, s_sem, r_sem, to)
        if when is None:
            copy.start()
        else:
            pl.when(when)(copy.start)
        sent.append((copy, when))

    def drain():
        for copy, when in sent:
            if when is None:
                copy.wait_send()
            else:
                pl.when(when)(copy.wait_send)
        sent.clear()

    def arrived(ref, sem, when=None):
        copy = remote(ref, ref, sem, sem, sibling)
        if when is None:
            copy.wait_recv()
        else:
            pl.when(when)(copy.wait_recv)

    anc_copy = pltpu.make_async_copy(anc_hbm, anc_ref, anc_sem)
    anc_copy.start()
    kv_local = {}
    for u in (0, 3):
        i = UNITS[u][1]
        for n, ref in enumerate((k_ref, v_ref)):
            copy = pltpu.make_async_copy(
                ref.at[:, lanes((r * 2 + i) * HD, HD)], kv[u].at[me[0], n, mine], kv_l.at[i, n])
            copy.start()
            kv_local[u, n] = copy
    q_local = pltpu.make_async_copy(q_ref.at[:, lanes(r * 2048, 2048)], q_s.at[0, mine], q_l.at[0])
    q_local.start()

    barrier = pltpu.get_barrier_semaphore()
    others = [dev(0, rows[0], col_at(0, 1)), dev(0, rows[0], col_at(0, 3))]
    others += [dev(0, lax.rem(rows[0] + d, 4), cols[0]) for d in (2, 1, 3)] + [*across, sibling]
    for partner in others:
        pl.semaphore_signal(barrier, inc=1, device_id=partner, device_id_type=MESH)
    pl.semaphore_wait(barrier, len(others))

    def share(u):
        b, i = UNITS[u]
        for n, ref in enumerate((k_ref, v_ref)):
            if b == 0:
                rr = x % 2 * 2 + 1 - c
                send(ref.at[:, lanes((rr * 2 + i) * HD, HD)], kv[u].at[me[0], n, mine],
                     kv_s.at[u, n, 0], kv_r.at[u, n, 0], sibling)
            else:
                for cc in range(2):
                    rr = px % 2 * 2 + cc
                    send(ref.at[:, lanes((rr * 2 + i) * HD, HD)], kv[u].at[me[0], n, mine],
                         kv_s.at[u, n, cc], kv_r.at[u, n, c], across[cc])

    def share_queries():
        for cc in range(2):
            rr = px % 2 * 2 + cc
            send(q_ref.at[:, lanes(rr * 2048, 2048)], q_s.at[1, mine], q_t.at[cc], q_r.at[c], across[cc])
        rr = x % 2 * 2 + 1 - c
        send(q_ref.at[:, lanes(rr * 2048, 2048)], q_s.at[0, mine], q_t.at[2], q_r.at[2], sibling)

    def own_ready(u):
        b, i = UNITS[u]
        for n in range(2):
            if b == 0:
                kv_local[u, n].wait()
                arrived(kv[u].at[me[0], n, theirs], kv_r.at[u, n, 0])
            else:
                for cc in range(2):
                    arrived(kv[u].at[me[1], n, pl.ds(cc * HALF, HALF)], kv_r.at[u, n, cc])

    def y_send(u, i):
        b = UNITS[u][0]
        block = kv[u].at[rows[b] * 4 + col_at(b, i)]
        for d in (1, 2, 3):
            send(block, block, ys.at[u, i, d - 1], yr.at[u, rows[b] * 4 + col_at(b, i)],
                 dev(b, lax.rem(rows[b] + d, 4), cols[b]), rows[b] + d < 4)

    def send_own(u):
        own_ready(u)
        b = UNITS[u][0]
        block = kv[u].at[me[b]]
        send(block, block, zs.at[u, 0], zr.at[u, 0], dev(b, rows[b], col_at(b, 1)))
        send(block, block, zs.at[u, 1], zr.at[u, 1], dev(b, rows[b], col_at(b, 3)))

    def z_near(u):
        b = UNITS[u][0]
        for n, i, to in ((0, 3, 1), (1, 1, 3)):
            block = kv[u].at[rows[b] * 4 + col_at(b, i)]
            arrived(block, zr.at[u, n])
            send(block.at[n], block.at[n], zf.at[u, n], zo.at[u, n], dev(b, rows[b], col_at(b, to)))
            y_send(u, i)

    def z_far(u):
        b = UNITS[u][0]
        block = kv[u].at[rows[b] * 4 + col_at(b, 2)]
        for n in range(2):
            arrived(block.at[n], zo.at[u, n])
        y_send(u, 2)

    def rest(u):
        b = UNITS[u][0]
        for row in range(3):
            for i in (0, 3, 1, 2):
                slot = row * 4 + col_at(b, i)
                arrived(kv[u].at[slot], yr.at[u, slot], rows[b] > row)

    places, listed = [], []

    def read_ancestors():
        anc_copy.wait()
        listed.extend([[anc_ref[x if b == 0 else px, i] for i in range(ANC)] for b in range(2)])
        for b in range(2):
            found = []
            for a in listed[b]:
                a0 = jnp.maximum(a, 0)
                ay, aw = a0 >> 6, (a0 >> 4) & 3
                ay = ay + fam[b] * (3 - 2 * ay)
                aw = aw + fam[b] * (3 - 2 * aw)
                found.append(jnp.where(a >= 0, ay * 4 + aw, me[b]))
            places.append(found + [me[b]])

    def build_bias():
        at_row = lax.broadcasted_iota(jnp.int32, (NODE, KEYS), 0)
        at = lax.broadcasted_iota(jnp.int32, (NODE, KEYS), 1)
        causal = jnp.where(at - ANC * NODE > at_row, -1e30, 0.0)
        for b in range(2):
            bias = causal
            for i, a in enumerate(listed[b]):
                inside = (at >= NODE * i) & (at < NODE * (i + 1))
                bias = jnp.where(inside, jnp.where(a >= 0, 0.0, -1e30), bias)
            bias_s[b] = bias

    out_copies = []

    def attend(u):
        b, i = UNITS[u]
        keys = jnp.concatenate([kv[u][s, 0] for s in places[b]], axis=0)
        values = jnp.concatenate([kv[u][s, 1] for s in places[b]], axis=0)
        for first in range(0, GROUP, JOINT):
            at = [(i * GROUP + first + j) * HD for j in range(JOINT)]
            queries = jnp.concatenate([q_s[b, :, a:a + HD] for a in at], axis=0)
            scores = lax.dot_general(queries, keys, (((1,), (1,)), ((), ())), preferred_element_type=jnp.float32)
            scores = (scores.reshape(JOINT, NODE, KEYS) + bias_s[b][None]).reshape(JOINT * NODE, KEYS)
            top = jnp.max(scores, axis=-1, keepdims=True)
            weights = jnp.exp2((scores - top) * EXP_SCALE)
            total = jnp.sum(weights, axis=-1, keepdims=True)
            mixed = jnp.dot(weights.astype(jnp.bfloat16), values, preferred_element_type=jnp.float32)
            mixed = (mixed / total).astype(jnp.bfloat16)
            for j in range(JOINT):
                o_s[u, :, (first + j) * HD:(first + j + 1) * HD] = mixed[j * NODE:(j + 1) * NODE]
        there = out_ref.at[:, lanes((r * 2 + i) * GROUP * HD, GROUP * HD)]
        if b == 0:
            copy = pltpu.make_async_copy(o_s.at[u, mine], there, o_l.at[i])
            copy.start()
            out_copies.append(copy)
            send(o_s.at[u, theirs], there, o_t.at[u, 0], o_r.at[2, i], sibling)
        else:
            for cc in range(2):
                send(o_s.at[u, pl.ds(cc * HALF, HALF)], there, o_t.at[u, cc], o_r.at[c, i], across[cc])

    share(0)
    share(1)
    share(2)
    share(3)
    share_queries()
    send_own(0)
    y_send(0, 0)
    send_own(1)
    y_send(1, 0)
    read_ancestors()
    build_bias()
    z_near(0)
    send_own(2)
    y_send(2, 0)
    z_near(1)
    z_far(0)
    send_own(3)
    y_send(3, 0)
    z_near(2)
    z_far(1)
    z_near(3)
    q_local.wait()
    arrived(q_s.at[0, theirs], q_r.at[2])
    rest(0)
    attend(0)
    z_far(2)
    for cc in range(2):
        arrived(q_s.at[1, pl.ds(cc * HALF, HALF)], q_r.at[cc])
    rest(1)
    attend(1)
    z_far(3)
    rest(2)
    attend(2)
    drain()
    rest(3)
    attend(3)
    drain()
    for copy in out_copies:
        copy.wait()
    for i in range(2):
        for n in range(3):
            arrived(out_ref.at[:, pl.ds(0, GROUP * HD)], o_r.at[n, i])


def local(queries, keys, values, ancestors):
    kv = pltpu.VMEM((16, 2, NODE, HD), jnp.bfloat16)
    dma = pltpu.SemaphoreType.DMA
    anywhere = pl.BlockSpec(memory_space=pl.ANY)
    return pl.pallas_call(
        kernel,
        out_shape=jax.ShapeDtypeStruct((HALF, 8192), jnp.bfloat16),
        in_specs=[anywhere] * 4,
        out_specs=anywhere,
        scratch_shapes=[
            pltpu.SMEM((4, ANC), jnp.int32), dma(()),
            kv, kv, kv, kv,
            pltpu.VMEM((2, NODE, 2048), jnp.bfloat16),
            pltpu.VMEM((4, NODE, 1024), jnp.bfloat16),
            pltpu.VMEM((2, NODE, KEYS), jnp.float32),
            dma((2, 2)), dma((4, 2, 2)), dma((4, 2, 2)), dma((1,)), dma((3,)), dma((3,)),
            dma((4, 2)), dma((4, 2)), dma((4, 2)), dma((4, 2)),
            dma((4, 4, 3)), dma((4, 16)),
            dma((2,)), dma((4, 2)), dma((3, 2)),
        ],
        compiler_params=pltpu.CompilerParams(
            collective_id=0, has_side_effects=True, vmem_limit_bytes=62 << 20),
        cost_estimate=pl.CostEstimate(
            flops=2 * 2 * 96 * 32 * 672 * 128, bytes_accessed=4 << 20, transcendentals=96 * 32 * 672),
        name="tree_attention",
    )(queries, keys, values, ancestors)


def solution(mesh):
    split = P(("dp", "tensor"), None)
    return jax.shard_map(
        local, mesh=mesh, in_specs=(split, split, split, P("dp", None)), out_specs=split, check_vma=False)
```

time: 71.3 us -> 60.2 us (0.84)
  the two profiles are of different devices: /device:TPU:11 before, /device:TPU:1 now
where the time goes in v2:
time: 60.2 us; the launch traced here: 60 us
  Pallas kernels  57.9 us (96%)
  local copies, waits for them, and re-layouts  2.06 us (3%)
    pallas_call x1, Pallas kernels, local(): pl.pallas_call(kernel, out_shape=jax.ShapeDtypeStruct((HALF, 8192), jnp.b...  57.9 us
    unnamed x1, local copies, waits for them, and re-layouts  2.06 us

profile of v2, /device:TPU:1, one launch (start us, length us, event | category | flops | bytes accessed | tf_op | source)
XLA Modules:
  0.0 60.0 jit_solution(16435539739924867609)
XLA Ops:
  0.0 57.9 %tree_attention.1 = bf16[48,8192]{1,0:T(8,128)(2,1)} custom-call(bf16[48,8192]{1,0:T(8,128)(2,1)} %q_ref.1, bf16[48,1024]{1,0:T(8,128)(2,1)} %k_ref.1, bf16[48,1024]{1,0:T(8,128)(2,1)} %v_ref.1, s32[4,6]{1,0:T(4,128)} %anc_hbm.1), custom_call_target="tpu_custom_call" | custom-call | flops 1056964608 | bytes 4194304 | tf_op jit(solution)/shard_map/tree_attention/pallas_call | solution.py:268
  57.9 2.1 %copy.6 = bf16[48,8192]{1,0:T(8,128)(2,1)} copy(bf16[48,8192]{1,0:T(8,128)(2,1)} %tree_attention.1) | data formatting | bytes 1572864

commit v3 on v2

--- a/solution.py
+++ b/solution.py
@@ -20,7 +20,7 @@
 
 
 def kernel(q_ref, k_ref, v_ref, anc_hbm, out_ref, anc_ref, anc_sem, kv0, kv1, kv2, kv3, q_s, o_s, bias_s,
-           kv_l, kv_s, kv_r, q_l, q_t, q_r, zs, zf, zr, zo, ys, yr, o_l, o_t, o_r):
+           kv_l, kv_s, kv_r, q_l, q_t, q_r, zs, zf, zr, zo, zd_s, zd_r, ys, yr, o_l, o_t, o_r):
     kv = (kv0, kv1, kv2, kv3)
     dp, t = lax.axis_index("dp"), lax.axis_index("tensor")
     x, c = t // 2, t % 2
@@ -91,7 +91,10 @@
     q_local.start()
 
     barrier = pltpu.get_barrier_semaphore()
-    others = [dev(0, rows[0], col_at(0, 1)), dev(0, rows[0], col_at(0, 3))]
+    others = []
+    for i in (1, 3):
+        there = dev(0, rows[0], col_at(0, i))[0]
+        others += [(there, t), (there, x * 2 + 1 - c)]
     others += [dev(0, lax.rem(rows[0] + d, 4), cols[0]) for d in (2, 1, 3)] + [*across, sibling]
     for partner in others:
         pl.semaphore_signal(barrier, inc=1, device_id=partner, device_id_type=MESH)
@@ -117,6 +120,15 @@
         rr = x % 2 * 2 + 1 - c
         send(q_ref.at[:, lanes(rr * 2048, 2048)], q_s.at[0, mine], q_t.at[2], q_r.at[2], sibling)
 
+    def send_raw():
+        for n, to in ((0, 1), (1, 3)):
+            there = dev(0, rows[0], col_at(0, to))[0]
+            for cc in range(2):
+                rr = x % 2 * 2 + cc
+                for m, ref in enumerate((k_ref, v_ref)):
+                    send(ref.at[:, lanes(rr * 2 * HD, HD)], kv[0].at[me[0], m, mine],
+                         zd_s.at[n, cc, m], zd_r.at[n, m, c], (there, x * 2 + cc))
+
     def own_ready(u):
         b, i = UNITS[u]
         for n in range(2):
@@ -134,20 +146,29 @@
             send(block, block, ys.at[u, i, d - 1], yr.at[u, rows[b] * 4 + col_at(b, i)],
                  dev(b, lax.rem(rows[b] + d, 4), cols[b]), rows[b] + d < 4)
 
-    def send_own(u):
-        own_ready(u)
+    def send_own(u, when=None):
         b = UNITS[u][0]
         block = kv[u].at[me[b]]
-        send(block, block, zs.at[u, 0], zr.at[u, 0], dev(b, rows[b], col_at(b, 1)))
-        send(block, block, zs.at[u, 1], zr.at[u, 1], dev(b, rows[b], col_at(b, 3)))
+        send(block, block, zs.at[u, 0], zr.at[u, 0], dev(b, rows[b], col_at(b, 1)), when)
+        send(block, block, zs.at[u, 1], zr.at[u, 1], dev(b, rows[b], col_at(b, 3)), when)
 
     def z_near(u):
         b = UNITS[u][0]
+        for n, i in ((0, 3), (1, 1)):
+            block = kv[u].at[rows[b] * 4 + col_at(b, i)]
+            if u == 0:
+                for m in range(2):
+                    for cc in range(2):
+                        arrived(block.at[m, pl.ds(cc * HALF, HALF)], zd_r.at[n, m, cc])
+            else:
+                arrived(block, zr.at[u, n])
+            y_send(u, i)
+
+    def z_pass(u):
+        b = UNITS[u][0]
         for n, i, to in ((0, 3, 1), (1, 1, 3)):
-            block = kv[u].at[rows[b] * 4 + col_at(b, i)]
-            arrived(block, zr.at[u, n])
-            send(block.at[n], block.at[n], zf.at[u, n], zo.at[u, n], dev(b, rows[b], col_at(b, to)))
-            y_send(u, i)
+            block = kv[u].at[rows[b] * 4 + col_at(b, i), n]
+            send(block, block, zf.at[u, n], zo.at[u, n], dev(b, rows[b], col_at(b, to)))
 
     def z_far(u):
         b = UNITS[u][0]
@@ -189,7 +210,14 @@
                 bias = jnp.where(inside, jnp.where(a >= 0, 0.0, -1e30), bias)
             bias_s[b] = bias
 
-    out_copies = []
+    def outputs(u):
+        b, i = UNITS[u]
+        there = out_ref.at[:, lanes((r * 2 + i) * GROUP * HD, GROUP * HD)]
+        if b == 0:
+            return (remote(o_s.at[u, theirs], there, o_t.at[u, 0], o_r.at[2, i], sibling),
+                    pltpu.make_async_copy(o_s.at[u, mine], there, o_l.at[i]))
+        return [remote(o_s.at[u, pl.ds(cc * HALF, HALF)], there, o_t.at[u, cc], o_r.at[c, i], across[cc])
+                for cc in range(2)]
 
     def attend(u):
         b, i = UNITS[u]
@@ -207,55 +235,65 @@
             mixed = (mixed / total).astype(jnp.bfloat16)
             for j in range(JOINT):
                 o_s[u, :, (first + j) * HD:(first + j + 1) * HD] = mixed[j * NODE:(j + 1) * NODE]
-        there = out_ref.at[:, lanes((r * 2 + i) * GROUP * HD, GROUP * HD)]
-        if b == 0:
-            copy = pltpu.make_async_copy(o_s.at[u, mine], there, o_l.at[i])
+        for copy in outputs(u):
             copy.start()
-            out_copies.append(copy)
-            send(o_s.at[u, theirs], there, o_t.at[u, 0], o_r.at[2, i], sibling)
-        else:
-            for cc in range(2):
-                send(o_s.at[u, pl.ds(cc * HALF, HALF)], there, o_t.at[u, cc], o_r.at[c, i], across[cc])
-
+
+    first = g == 0
+    send_raw()
     share(0)
     share(1)
     share(2)
     share(3)
     share_queries()
-    send_own(0)
+    own_ready(0)
     y_send(0, 0)
+    own_ready(1)
     send_own(1)
     y_send(1, 0)
+    own_ready(2)
+    send_own(2, first)
+    own_ready(3)
+    send_own(3, first)
     read_ancestors()
     build_bias()
     z_near(0)
-    send_own(2)
+    send_own(2, jnp.logical_not(first))
     y_send(2, 0)
     z_near(1)
-    z_far(0)
-    send_own(3)
+    z_pass(1)
+    send_own(3, jnp.logical_not(first))
     y_send(3, 0)
     z_near(2)
+    z_pass(2)
     z_far(1)
+    z_pass(0)
     z_near(3)
-    q_local.wait()
-    arrived(q_s.at[0, theirs], q_r.at[2])
-    rest(0)
-    attend(0)
+    z_pass(3)
     z_far(2)
     for cc in range(2):
         arrived(q_s.at[1, pl.ds(cc * HALF, HALF)], q_r.at[cc])
     rest(1)
     attend(1)
-    z_far(3)
+    z_far(0)
+    q_local.wait()
+    arrived(q_s.at[0, theirs], q_r.at[2])
+    pl.when(rows[0] == 0)(lambda: attend(0))
     rest(2)
     attend(2)
+    z_far(3)
+    rest(0)
+    pl.when(rows[0] > 0)(lambda: attend(0))
     drain()
     rest(3)
     attend(3)
     drain()
-    for copy in out_copies:
-        copy.wait()
+    for u in range(4):
+        first_copy, second_copy = outputs(u)
+        first_copy.wait_send()
+        if UNITS[u][0] == 0:
+            second_copy.wait()
+        else:
+            second_copy.wait_send()
     for i in range(2):
         for n in range(3):
             arrived(out_ref.at[:, pl.ds(0, GROUP * HD)], o_r.at[n, i])
@@ -277,7 +315,7 @@
             pltpu.VMEM((4, NODE, 1024), jnp.bfloat16),
             pltpu.VMEM((2, NODE, KEYS), jnp.float32),
             dma((2, 2)), dma((4, 2, 2)), dma((4, 2, 2)), dma((1,)), dma((3,)), dma((3,)),
-            dma((4, 2)), dma((4, 2)), dma((4, 2)), dma((4, 2)),
+            dma((4, 2)), dma((4, 2)), dma((4, 2)), dma((4, 2)), dma((2, 2, 2)), dma((2, 2, 2)),
             dma((4, 4, 3)), dma((4, 16)),
             dma((2,)), dma((4, 2)), dma((3, 2)),
         ],

time: 60.2 us -> 57.7 us (0.958)
  Pallas kernels: 57.9 us -> 55.5 us
    pallas_call x1, Pallas kernels: 57.9 us -> 55.5 us  [local(): pl.pallas_call(kernel, out_shape=jax.ShapeDtypeStruct((HALF, 8192), jnp.b...]
where the time goes in v3:
time: 57.7 us; the launch traced here: 57.5 us
  Pallas kernels  55.5 us (96%)
  local copies, waits for them, and re-layouts  2.06 us (4%)
    pallas_call x1, Pallas kernels, local(): pl.pallas_call(kernel, out_shape=jax.ShapeDtypeStruct((HALF, 8192), jnp.b...  55.5 us
    unnamed x1, local copies, waits for them, and re-layouts  2.06 us

profile of v3, /device:TPU:1, one launch (start us, length us, event | category | flops | bytes accessed | tf_op | source)
XLA Modules:
  0.0 57.5 jit_solution(9675062137598122800)
XLA Ops:
  0.0 55.5 %tree_attention.1 = bf16[48,8192]{1,0:T(8,128)(2,1)} custom-call(bf16[48,8192]{1,0:T(8,128)(2,1)} %q_ref.1, bf16[48,1024]{1,0:T(8,128)(2,1)} %k_ref.1, bf16[48,1024]{1,0:T(8,128)(2,1)} %v_ref.1, s32[4,6]{1,0:T(4,128)} %anc_hbm.1), custom_call_target="tpu_custom_call" | custom-call | flops 1056964608 | bytes 4194304 | tf_op jit(solution)/shard_map/tree_attention/pallas_call | solution.py:306
  55.5 2.1 %copy.6 = bf16[48,8192]{1,0:T(8,128)(2,1)} copy(bf16[48,8192]{1,0:T(8,128)(2,1)} %tree_attention.1) | data formatting | bytes 1572864

commit v4 on v3

--- a/solution.py
+++ b/solution.py
@@ -305,7 +305,7 @@
     anywhere = pl.BlockSpec(memory_space=pl.ANY)
     return pl.pallas_call(
         kernel,
-        out_shape=jax.ShapeDtypeStruct((HALF, 8192), jnp.bfloat16),
+        out_shape=pltpu.VMEM((HALF, 8192), jnp.bfloat16),
         in_specs=[anywhere] * 4,
         out_specs=anywhere,
         scratch_shapes=[

time: 57.7 us -> 56.3 us (0.976)
  local copies, waits for them, and re-layouts: 2.06 us -> 0.88 us
    unnamed x1, local copies, waits for them, and re-layouts: 2.06 us -> 0.88 us
where the time goes in v4:
time: 56.3 us; the launch traced here: 56.2 us
  Pallas kernels  55.3 us (98%)
  local copies, waits for them, and re-layouts  0.88 us (2%)
    pallas_call x1, Pallas kernels, local(): pl.pallas_call(kernel, out_shape=pltpu.VMEM((HALF, 8192), jnp.bfloat16),...  55.3 us

profile of v4, /device:TPU:1, one launch (start us, length us, event | category | flops | bytes accessed | tf_op | source)
XLA Modules:
  0.0 56.2 jit_solution(12378890666054386799)
XLA Ops:
  0.0 55.3 %tree_attention.1 = bf16[48,8192]{1,0:T(8,128)(2,1)S(1)} custom-call(bf16[48,8192]{1,0:T(8,128)(2,1)} %q_ref.1, bf16[48,1024]{1,0:T(8,128)(2,1)} %k_ref.1, bf16[48,1024]{1,0:T(8,128)(2,1)} %v_ref.1, s32[4,6]{1,0:T(4,128)} %anc_hbm.1), custom_call_target="tpu_custom_call" | custom-call | flops 1056964608 | bytes 4194304 | tf_op jit(solution)/shard_map/tree_attention/pallas_call | solution.py:306
  55.4 0.9 %copy.6 = bf16[48,8192]{1,0:T(8,128)(2,1)} copy(bf16[48,8192]{1,0:T(8,128)(2,1)S(1)} %tree_attention.1) | data formatting | bytes 1572864

commit v5 on v4

--- a/solution.py
+++ b/solution.py
@@ -154,7 +154,7 @@
 
     def z_near(u):
         b = UNITS[u][0]
-        for n, i in ((0, 3), (1, 1)):
+        for n, i, to in ((0, 3, 1), (1, 1, 3)):
             block = kv[u].at[rows[b] * 4 + col_at(b, i)]
             if u == 0:
                 for m in range(2):
@@ -163,12 +163,17 @@
             else:
                 arrived(block, zr.at[u, n])
             y_send(u, i)
+            if u:
+                pass_half(u, n, i, to)
+
+    def pass_half(u, n, i, to):
+        b = UNITS[u][0]
+        block = kv[u].at[rows[b] * 4 + col_at(b, i), n]
+        send(block, block, zf.at[u, n], zo.at[u, n], dev(b, rows[b], col_at(b, to)))
 
     def z_pass(u):
-        b = UNITS[u][0]
         for n, i, to in ((0, 3, 1), (1, 1, 3)):
-            block = kv[u].at[rows[b] * 4 + col_at(b, i), n]
-            send(block, block, zf.at[u, n], zo.at[u, n], dev(b, rows[b], col_at(b, to)))
+            pass_half(u, n, i, to)
 
     def z_far(u):
         b = UNITS[u][0]
@@ -238,7 +243,7 @@
         for copy in outputs(u):
             copy.start()
 
-    first = g == 0
+    first = (g == 0) & (w > 0)
     send_raw()
     share(0)
     share(1)
@@ -260,15 +265,12 @@
     send_own(2, jnp.logical_not(first))
     y_send(2, 0)
     z_near(1)
-    z_pass(1)
     send_own(3, jnp.logical_not(first))
     y_send(3, 0)
     z_near(2)
-    z_pass(2)
     z_far(1)
     z_pass(0)
     z_near(3)
-    z_pass(3)
     z_far(2)
     for cc in range(2):
         arrived(q_s.at[1, pl.ds(cc * HALF, HALF)], q_r.at[cc])

time: 56.3 us -> 56 us (level)
  the two profiles are of different devices: /device:TPU:1 before, /device:TPU:67 now
where the time goes in v5:
time: 56 us; the launch traced here: 55.9 us
  Pallas kernels  55 us (98%)
  local copies, waits for them, and re-layouts  0.88 us (2%)
    pallas_call x1, Pallas kernels, local(): pl.pallas_call(kernel, out_shape=pltpu.VMEM((HALF, 8192), jnp.bfloat16),...  55 us

profile of v5, /device:TPU:67, one launch (start us, length us, event | category | flops | bytes accessed | tf_op | source)
XLA Modules:
  0.0 55.9 jit_solution(14321701847526382824)
XLA Ops:
  0.0 55.0 %tree_attention.1 = bf16[48,8192]{1,0:T(8,128)(2,1)S(1)} custom-call(bf16[48,8192]{1,0:T(8,128)(2,1)} %q_ref.1, bf16[48,1024]{1,0:T(8,128)(2,1)} %k_ref.1, bf16[48,1024]{1,0:T(8,128)(2,1)} %v_ref.1, s32[4,6]{1,0:T(4,128)} %anc_hbm.1), custom_call_target="tpu_custom_call" | custom-call | flops 1056964608 | bytes 4194304 | tf_op jit(solution)/shard_map/tree_attention/pallas_call | solution.py:308
  55.0 0.9 %copy.6 = bf16[48,8192]{1,0:T(8,128)(2,1)} copy(bf16[48,8192]{1,0:T(8,128)(2,1)S(1)} %tree_attention.1) | data formatting | bytes 1572864

commit v6 on v5

--- a/solution.py
+++ b/solution.py
@@ -120,6 +120,12 @@
         rr = x % 2 * 2 + 1 - c
         send(q_ref.at[:, lanes(rr * 2048, 2048)], q_s.at[0, mine], q_t.at[2], q_r.at[2], sibling)
 
+    def needed(b, skipped):
+        skip = cols[b] == skipped[0]
+        for col in skipped[1:]:
+            skip = skip | (cols[b] == col)
+        return jnp.logical_not((rows[b] == 3) & skip)
+
     def send_raw():
         for n, to in ((0, 1), (1, 3)):
             there = dev(0, rows[0], col_at(0, to))[0]
@@ -127,7 +133,8 @@
                 rr = x % 2 * 2 + cc
                 for m, ref in enumerate((k_ref, v_ref)):
                     send(ref.at[:, lanes(rr * 2 * HD, HD)], kv[0].at[me[0], m, mine],
-                         zd_s.at[n, cc, m], zd_r.at[n, m, c], (there, x * 2 + cc))
+                         zd_s.at[n, cc, m], zd_r.at[n, m, c], (there, x * 2 + cc),
+                         needed(0, (3,)) if n == 0 else None)
 
     def own_ready(u):
         b, i = UNITS[u]
@@ -149,7 +156,9 @@
     def send_own(u, when=None):
         b = UNITS[u][0]
         block = kv[u].at[me[b]]
-        send(block, block, zs.at[u, 0], zr.at[u, 0], dev(b, rows[b], col_at(b, 1)), when)
+        kept = needed(b, (3,))
+        send(block, block, zs.at[u, 0], zr.at[u, 0], dev(b, rows[b], col_at(b, 1)),
+             kept if when is None else when & kept)
         send(block, block, zs.at[u, 1], zr.at[u, 1], dev(b, rows[b], col_at(b, 3)), when)
 
     def z_near(u):
@@ -159,9 +168,10 @@
             if u == 0:
                 for m in range(2):
                     for cc in range(2):
-                        arrived(block.at[m, pl.ds(cc * HALF, HALF)], zd_r.at[n, m, cc])
+                        arrived(block.at[m, pl.ds(cc * HALF, HALF)], zd_r.at[n, m, cc],
+                                needed(b, (0,)) if n == 0 else None)
             else:
-                arrived(block, zr.at[u, n])
+                arrived(block, zr.at[u, n], needed(b, (0,)) if n == 0 else None)
             y_send(u, i)
             if u:
                 pass_half(u, n, i, to)
@@ -169,7 +179,8 @@
     def pass_half(u, n, i, to):
         b = UNITS[u][0]
         block = kv[u].at[rows[b] * 4 + col_at(b, i), n]
-        send(block, block, zf.at[u, n], zo.at[u, n], dev(b, rows[b], col_at(b, to)))
+        send(block, block, zf.at[u, n], zo.at[u, n], dev(b, rows[b], col_at(b, to)),
+             needed(b, (0, 3)) if n == 0 else None)
 
     def z_pass(u):
         for n, i, to in ((0, 3, 1), (1, 1, 3)):
@@ -179,7 +190,7 @@
         b = UNITS[u][0]
         block = kv[u].at[rows[b] * 4 + col_at(b, 2)]
         for n in range(2):
-            arrived(block.at[n], zo.at[u, n])
+            arrived(block.at[n], zo.at[u, n], needed(b, (0, 1)) if n == 0 else None)
         y_send(u, 2)
 
     def rest(u):

time: 56 us -> 55.8 us (level)
  the two profiles are of different devices: /device:TPU:67 before, /device:TPU:113 now
where the time goes in v6:
time: 55.8 us; the launch traced here: 55.7 us
  Pallas kernels  54.8 us (98%)
  local copies, waits for them, and re-layouts  0.88 us (2%)
    pallas_call x1, Pallas kernels, local(): pl.pallas_call(kernel, out_shape=pltpu.VMEM((HALF, 8192), jnp.bfloat16),...  54.8 us

profile of v6, /device:TPU:113, one launch (start us, length us, event | category | flops | bytes accessed | tf_op | source)
XLA Modules:
  0.0 55.7 jit_solution(55435270919640170)
XLA Ops:
  0.0 54.8 %tree_attention.1 = bf16[48,8192]{1,0:T(8,128)(2,1)S(1)} custom-call(bf16[48,8192]{1,0:T(8,128)(2,1)} %q_ref.1, bf16[48,1024]{1,0:T(8,128)(2,1)} %k_ref.1, bf16[48,1024]{1,0:T(8,128)(2,1)} %v_ref.1, s32[4,6]{1,0:T(4,128)} %anc_hbm.1), custom_call_target="tpu_custom_call" | custom-call | flops 1056964608 | bytes 4194304 | tf_op jit(solution)/shard_map/tree_attention/pallas_call | solution.py:319
  54.9 0.9 %copy.6 = bf16[48,8192]{1,0:T(8,128)(2,1)} copy(bf16[48,8192]{1,0:T(8,128)(2,1)S(1)} %tree_attention.1) | data formatting | bytes 1572864
